TPU v7x, 32 devices: a whole 2x2x4 slice. The times are simulated.
32 devices in a mesh: grp: 4 (over y, x), ing: 8 (over z, core).
Axes of the slice: x: 2, y: 2, z: 4, core: 2. Of those that a mesh axis runs over, the one named last changes fastest.
Arguments:
- tokens: bfloat16 [4096, 14848], P(('grp', 'ing')), may hold values from -6 to 6
- ln_gain: float32 [14848], replicated, may hold values from 0.1 to 1.9
- ln_bias: float32 [14848], replicated, may hold values from -3 to 3
- master: float32 [14848, 512], P(('ing', 'grp')), may hold values from -0.046875 to 0.046875
- grad: bfloat16 [14848, 512], P(('ing', 'grp')), may hold values from -6 to 6
- moment1: float32 [14848, 512], P(('ing', 'grp')), may hold values from -0.6 to 0.6
- moment2: float32 [14848, 512], P(('ing', 'grp')), may hold values from 0.02 to 0.2
Outputs:
- new_master: float32 [14848, 512], P(('ing', 'grp'))
- new_moment1: float32 [14848, 512], P(('ing', 'grp'))
- new_moment2: float32 [14848, 512], P(('ing', 'grp'))
- keys: bfloat16 [4096, 512], P(('grp', 'ing'))
All inputs are finite; a program needn't handle non-finite values.
Results may differ from a plain program's by a relative error of at most 0.012.
Values may be sent and summed in bfloat16 or wider, within the bound.
A program may use at most 128 MiB of HBM per device.

v0:
```python
import jax
import jax.numpy as jnp
from jax import lax
from jax.sharding import PartitionSpec as P

QBLOCK = 128


def expand_rows(values, scales):
    count = values.shape[0]
    blocks = scales.shape[1]
    full = (
        values.astype(jnp.float32).reshape(count, blocks, -1)
        * scales.astype(jnp.float32)[:, :, None]
    )
    return full.reshape(count, -1).astype(jnp.bfloat16)


def shards(tokens, ln_gain, ln_bias, master, grad, moment1, moment2):
    gradient = grad.astype(jnp.float32)
    new_moment1 = 0.9 * moment1 + 0.1 * gradient
    new_moment2 = 0.95 * moment2 + 0.05 * gradient * gradient
    step_size = new_moment1 / 0.19 / (jnp.sqrt(new_moment2 / 0.0975) + 1e-08)
    new_master = master - 0.008 * (step_size + 0.1 * master)
    own_rows, width = new_master.shape
    blocked = new_master.reshape(own_rows, width // QBLOCK, QBLOCK)
    scale = ((jnp.max(jnp.abs(blocked), axis=2) + 1e-06) / 127.0).astype(jnp.bfloat16)
    quant = (
        (blocked / scale.astype(jnp.float32)[:, :, None])
        .astype(jnp.bfloat16)
        .reshape(own_rows, width)
    )
    values = tokens.astype(jnp.float32)
    mean = jnp.mean(values, axis=1, keepdims=True)
    centered = values - mean
    var = jnp.mean(centered * centered, axis=1, keepdims=True)
    normed = (centered * lax.rsqrt(var + 1e-05) * ln_gain + ln_bias).astype(jnp.bfloat16)
    group_values, group_scales = (
        lax.all_gather(quant, "grp", axis=0, tiled=True),
        lax.all_gather(scale, "grp", axis=0, tiled=True),
    )
    weight_rows = expand_rows(group_values, group_scales)
    gathered = lax.all_to_all(normed, "ing", split_axis=1, concat_axis=0, tiled=True)
    summed = lax.psum_scatter(
        jnp.dot(gathered, weight_rows, preferred_element_type=jnp.float32),
        "ing",
        scatter_dimension=0,
        tiled=True,
    )
    result = summed.astype(jnp.bfloat16)
    return (new_master, new_moment1, new_moment2, result)


def solution(mesh):
    in_specs = (
        P(("grp", "ing"), None),
        P(),
        P(),
        P(("ing", "grp"), None),
        P(("ing", "grp"), None),
        P(("ing", "grp"), None),
        P(("ing", "grp"), None),
    )
    out_specs = (
        P(("ing", "grp"), None),
        P(("ing", "grp"), None),
        P(("ing", "grp"), None),
        P(("grp", "ing"), None),
    )
    return jax.shard_map(shards, mesh=mesh, in_specs=in_specs, out_specs=out_specs, check_vma=False)
```

profile of v0, /device:TPU:0, one launch (start us, length us, event | category | flops | bytes accessed | tf_op | source)
XLA Modules:
  0.0 173.5 jit_solution(883897485082422040)
XLA Ops:
  7.2 6.1 %copy.21 = bf16[128,14848]{0,1:T(8,128)(2,1)} copy(bf16[128,14848]{1,0:T(8,128)(2,1)} %param.7) | data formatting | bytes 7602176 | tf_op args[0]
  13.3 0.0 copy-start
  13.3 0.0 copy-start.4
  13.3 0.0 copy-start.5
  13.3 3.6 %convert_reduce_fusion = f32[128]{0:T(128)S(1)} fusion(bf16[128,14848]{0,1:T(8,128)(2,1)} %copy.21), kind=kLoop, calls=%fused_computation.1 | loop fusion | flops 3800960 | bytes 3801600 | tf_op jit(solution)/shard_map/reduce_sum | solution.py:34
  16.9 0.0 copy-done
  17.0 2.0 %fusion.2 = f32[128]{0:T(128)S(1)} fusion(bf16[128,14848]{0,1:T(8,128)(2,1)S(1)} %copy-done, f32[128]{0:T(128)S(1)} %broadcast_multiply_fusion), kind=kLoop, calls=%fused_computation.4 | loop fusion | flops 7602048 | bytes 3802112 | tf_op jit(solution)/shard_map/reduce_sum | solution.py:36
  19.0 0.0 copy-done.4
  19.0 0.0 copy-done.5
  19.0 9.0 %fusion.5 = bf16[128,14848]{0,1:T(8,128)(2,1)} fusion(bf16[128,14848]{0,1:T(8,128)(2,1)S(1)} %copy-done, f32[14848]{0:T(1024)S(1)} %copy-done.4, f32[14848]{0:T(1024)S(1)} %copy-done.5, f32[128]{0:T(128)S(1)} %add_rsqrt_fusion, f32[128]{0:T(128)S(1)} %broadcast_multiply_fusion), kind=kLoop, calls=%fused_computation.7 | loop fusion | flops 11403264 | bytes 7721984 | tf_op jit(solution)/shard_map/convert_element_type | solution.py:37
  28.0 0.0 copy-start.2
  28.0 0.0 copy-start.3
  28.0 6.5 %all-to-all-start = ((bf16[128,8,1856]{0,2,1:T(8,128)(2,1)}), bf16[128,8,1856]{0,2,1:T(8,128)(2,1)}, u32[]{:S(2)}, u32[]{:S(2)}) async-start(bf16[128,8,1856]{0,2,1:T(8,128)(2,1)} %bitcast.23), calls=%async_computation | async-start | bytes 7602176 | tf_op jit(solution)/shard_map/all_to_all | solution.py:43
  34.4 0.0 all-gather.3.cloned.1.call-start
  34.5 0.0 copy-done.2
  34.5 0.0 copy-done.3
  34.5 3.5 %fusion.16 = (f32[464,512]{1,0:T(8,128)S(1)}, f32[464,512]{1,0:T(8,128)S(1)}, f32[464,512]{1,0:T(8,128)}, f32[464,512]{1,0:T(8,128)}) fusion(f32[464,512]{1,0:T(8,128)S(1)} %copy-done.2, bf16[464,512]{1,0:T(8,128)(2,1)S(1)} %copy-done.3, f32[464,512]{1,0:T(8,128)} %param.12, f32[464,512]{1,0:T(8,128)} %param.13), kind=kLoop, calls=%fused_computation.25 | loop fusion | flops 4038656 | bytes 7127040 | tf_op jit(solution)/shard_map/abs | solution.py:27
  38.0 0.0 copy-start.1
  38.0 0.3 abs.7
  38.3 0.6 reduce_max.9
  38.9 0.5 div.47
  39.5 1.0 fusion.13
  40.5 0.0 all-gather.3.cloned.1.call-update
  40.5 0.0 copy-done.1
  40.5 0.0 reduce-scatter.2.cloned.1.call-start
  40.5 0.1 copy.23
  40.6 8.2 %all-gather = bf16[4,464,4]{1,2,0:T(4,128)(2,1)S(1)} all-gather(bf16[1,464,4]{1,2,0:T(4,128)(2,1)S(1)} %copy.23), channel_id=1, replica_groups=mesh['grp'=4,'ing'=8] {'grp'}, dimensions={0}, use_global_device_ids=true | all-gather | bytes 18560 | tf_op jit(solution)/shard_map/all_gather | solution.py:40
  48.8 0.2 copy.26
  49.1 26.7 %all-gather.3.cloned.1.call-done = bf16[1856,512]{1,0:T(8,128)(2,1)} async-done(((bf16[464,512]{1,0:T(8,128)(2,1)}), bf16[1856,512]{1,0:T(8,128)(2,1)}) %all-gather.3.cloned.1.call-update) | async-done | bytes 1900560 | tf_op jit(solution)/shard_map/all_gather | solution.py:39
  75.7 0.0 copy-start.6
  75.8 44.4 %all-to-all-done = bf16[128,8,1856]{0,2,1:T(8,128)(2,1)} async-done(((bf16[128,8,1856]{0,2,1:T(8,128)(2,1)}), bf16[128,8,1856]{0,2,1:T(8,128)(2,1)}, u32[]{:S(2)}, u32[]{:S(2)}) %all-to-all-start) | async-done | bytes 3801120 | tf_op jit(solution)/shard_map/all_to_all | solution.py:43
  120.1 4.3 %mul.79 = f32[1856,4,128]{2,1,0:T(4,128)S(1)} broadcast(f32[1856,4]{1,0:T(8,128)S(1)} %bitcast.24), dimensions={0,1} | broadcast | bytes 3830784 | tf_op jit(solution)/shard_map/mul | solution.py:13
  124.4 0.0 copy-done.6
  124.4 5.8 %fusion.7 = f32[1024,512]{1,0:T(8,128)} fusion(f32[232,8,4,128]{3,2,1,0:T(4,128)S(1)} %bitcast.26, bf16[1856,512]{1,0:T(8,128)(2,1)S(1)} %copy-done.6, bf16[128,8,1856]{0,2,1:T(8,128)(2,1)} %all-to-all-done), kind=kOutput, calls=%fused_computation.10 | convolution fusion | flops 1949007872 | bytes 11599872 | tf_op jit(solution)/shard_map/dot_general | solution.py:45
  130.2 0.0 reduce-scatter.2.cloned.1.call-update
  130.2 34.9 %reduce-scatter.2.cloned.1.call-done = f32[128,512]{1,0:T(8,128)} async-done(((f32[1024,512]{1,0:T(8,128)}), f32[128,512]{1,0:T(8,128)}) %reduce-scatter.2.cloned.1.call-update) | async-done | bytes 262160 | tf_op jit(solution)/shard_map/reduce_scatter | solution.py:44
  165.1 1.6 convert_element_type.48
  (3 shorter events, 0.1 us)
Async XLA Ops:
  13.3 3.7 %copy-start = (bf16[128,14848]{0,1:T(8,128)(2,1)S(1)}, bf16[128,14848]{0,1:T(8,128)(2,1)}, u32[]{:S(2)}) copy-start(bf16[128,14848]{0,1:T(8,128)(2,1)} %copy.21) | copy-start | bytes 11403268
  13.3 5.7 %copy-start.4 = (f32[14848]{0:T(1024)S(1)}, f32[14848]{0:T(1024)}, u32[]{:S(2)}) copy-start(f32[14848]{0:T(1024)} %param.9) | copy-start | bytes 178180
  13.3 5.7 %copy-start.5 = (f32[14848]{0:T(1024)S(1)}, f32[14848]{0:T(1024)}, u32[]{:S(2)}) copy-start(f32[14848]{0:T(1024)} %param.8) | copy-start | bytes 178180
  28.0 6.5 %copy-start.2 = (f32[464,512]{1,0:T(8,128)S(1)}, f32[464,512]{1,0:T(8,128)}, u32[]{:S(2)}) copy-start(f32[464,512]{1,0:T(8,128)} %param.10) | copy-start | bytes 2850820
  28.0 6.5 %copy-start.3 = (bf16[464,512]{1,0:T(8,128)(2,1)S(1)}, bf16[464,512]{1,0:T(8,128)(2,1)}, u32[]{:S(2)}) copy-start(bf16[464,512]{1,0:T(8,128)(2,1)} %param.11) | copy-start | bytes 1425412
  28.0 92.1 %all-to-all-start = ((bf16[128,8,1856]{0,2,1:T(8,128)(2,1)}), bf16[128,8,1856]{0,2,1:T(8,128)(2,1)}, u32[]{:S(2)}, u32[]{:S(2)}) async-start(bf16[128,8,1856]{0,2,1:T(8,128)(2,1)} %bitcast.23), calls=%async_computation | async-start | bytes 7602176 | tf_op jit(solution)/shard_map/all_to_all | solution.py:43
  34.4 41.3 %all-gather.3.cloned.1.call-start = ((), (), s32[]{:S(2)}) async-start(), calls=%async_computation.2 | async-start | bytes 2375680 | tf_op jit(solution)/shard_map/all_gather | solution.py:39
  38.0 2.5 %copy-start.1 = (f32[464,512]{1,0:T(8,128)}, f32[464,512]{1,0:T(8,128)S(1)}, u32[]{:S(2)}) copy-start(f32[464,512]{1,0:T(8,128)S(1)} %get-tuple-element.5) | copy-start | bytes 2850820
  40.5 124.6 %reduce-scatter.2.cloned.1.call-start = ((), (), s32[]{:S(2)}) async-start(), calls=%async_computation.3 | async-start | bytes 2359296 | tf_op jit(solution)/shard_map/reduce_scatter | solution.py:44
  75.7 48.6 %copy-start.6 = (bf16[1856,512]{1,0:T(8,128)(2,1)S(1)}, bf16[1856,512]{1,0:T(8,128)(2,1)}, u32[]{:S(2)}) copy-start(bf16[1856,512]{1,0:T(8,128)(2,1)} %all-gather.3.cloned.1.call-done) | copy-start | bytes 5701636
Sparse Core Ops, SparseCore 0:
  40.6 35.0 all-gather.2
  130.3 34.7 reduce-scatter.1
where the time goes:
time: 174 us
  waiting for transfers between devices  106 us (61%)
  other arithmetic  21.3 us (12%)
  between operations  14.1 us (8%)
  local copies, waits for them, and re-layouts  11.6 us (7%)
  blocking collectives  8.17 us (5%)
  starting transfers between devices  6.54 us (4%)
  matrix products  5.77 us (3%)
    all_to_all x1, waiting for transfers between devices, shards(): lax.all_to_all(normed, 'ing', split_axis=1, concat_axis=0, tiled=True)  44.4 us
    reduce_scatter x1, waiting for transfers between devices, shards(): lax.psum_scatter(jnp.dot(gathered, weight_rows, preferred_element_type=jn...  34.9 us
    all_gather x1, waiting for transfers between devices, shards(): lax.all_gather(quant, 'grp', axis=0, tiled=True)  26.7 us
    convert_element_type x1, other arithmetic, shards(): (centered * lax.rsqrt(var + 1e-05) * ln_gain + ln_bias).astype(jnp.bfloat16)  8.98 us
    all_gather x1, blocking collectives, shards(): lax.all_gather(scale, 'grp', axis=0, tiled=True)  8.17 us
    all_to_all x1, starting transfers between devices, shards(): lax.all_to_all(normed, 'ing', split_axis=1, concat_axis=0, tiled=True)  6.46 us
    unnamed x16, local copies, waits for them, and re-layouts  6.25 us
    dot_general x1, matrix products, shards(): jnp.dot(gathered, weight_rows, preferred_element_type=jnp.float32)  5.77 us
  transfers between devices with their start and end apart: 3, of which 3 were waited for; matrix products, arithmetic and copies ran while one was open for 4% of the time, Pallas kernels for 0%

commit v1 on v0

--- a/solution.py
+++ b/solution.py
@@ -1,9 +1,15 @@
+import functools
+
 import jax
 import jax.numpy as jnp
 from jax import lax
+from jax.experimental import pallas as pl
+from jax.experimental.pallas import tpu as pltpu
 from jax.sharding import PartitionSpec as P
 
 QBLOCK = 128
+MESH = pl.DeviceIdType.MESH
+LANES = 512
 
 
 def expand_rows(values, scales):
@@ -51,7 +57,332 @@
     return (new_master, new_moment1, new_moment2, result)
 
 
+def adam_kernel(master, grad, moment1, moment2, out_master, out_m1, out_m2, weight):
+    gradient = grad[...].astype(jnp.float32)
+    old = master[...]
+    first = 0.9 * moment1[...] + 0.1 * gradient
+    second = 0.95 * moment2[...] + 0.05 * gradient * gradient
+    step_size = first / 0.19 / (jnp.sqrt(second / 0.0975) + 1e-08)
+    updated = old - 0.008 * (step_size + 0.1 * old)
+    out_master[...] = updated
+    out_m1[...] = first
+    out_m2[...] = second
+    largest = jnp.max(jnp.abs(updated), axis=1, keepdims=True)
+    scale = ((largest + 1e-06) / 127.0).astype(jnp.bfloat16).astype(jnp.float32)
+    quant = (updated / scale).astype(jnp.bfloat16)
+    weight[...] = (quant.astype(jnp.float32) * scale).astype(jnp.bfloat16)
+
+
+def adam(master, grad, moment1, moment2):
+    rows, width = master.shape
+    block = pl.BlockSpec((rows, QBLOCK), lambda i: (0, i))
+    wide = jax.ShapeDtypeStruct((rows, width), jnp.float32)
+    return pl.pallas_call(
+        adam_kernel,
+        grid=(width // QBLOCK,),
+        in_specs=[block] * 4,
+        out_specs=[block] * 4,
+        out_shape=[wide, wide, wide, jax.ShapeDtypeStruct((rows, width), jnp.bfloat16)],
+        compiler_params=pltpu.CompilerParams(vmem_limit_bytes=32 * 2**20),
+    )(master, grad, moment1, moment2)
+
+
+def gather_kernel(
+    grps, rows, planes, cuts,
+    weight, tokens, gain, bias, keys,
+    full, tok, norm, acc, part,
+    local_sem, recv_sem, send_sem, side_recv, side_send,
+):
+    cut_c, cut_a, cut_b = cuts
+    g = lax.axis_index("grp")
+    i = lax.axis_index("ing")
+    z, k = i // 2, i % 2
+    gx, gy = g + 1 - 2 * (g % 2), lax.rem(g + 2, 4)
+    gxy = gy + 1 - 2 * (gy % 2)
+    half = 4 * rows
+    plane = 2 * half
+    window = (half + 127) // 128 * 128
+    shift = plane - window
+    count, features = tokens.shape
+    top = planes - 1
+
+    fetch_w = pltpu.make_async_copy(
+        weight, full.at[pl.ds(pl.multiple_of((i * 4 + g) * rows, 16), rows), :], local_sem.at[0])
+    fetch_w.start()
+    fetch_t = pltpu.make_async_copy(tokens, tok, local_sem.at[1])
+    fetch_t.start()
+
+    barrier = pltpu.get_barrier_semaphore()
+    for peer in ((gx, i), (gy, i), (g, i + 1 - 2 * k)):
+        pl.semaphore_signal(barrier, inc=1, device_id=peer, device_id_type=MESH)
+
+    @pl.when(z < top)
+    def _():
+        pl.semaphore_signal(barrier, inc=1, device_id=(g, i + 2), device_id_type=MESH)
+
+    @pl.when(z > 0)
+    def _():
+        pl.semaphore_signal(barrier, inc=1, device_id=(g, i - 2), device_id_type=MESH)
+
+    gap = window - half
+    if gap:
+        for p in range(planes):
+            at = pl.multiple_of(p * plane + half - gap * k, 16)
+            full[pl.ds(at, gap), :] = jnp.zeros((gap, full.shape[1]), full.dtype)
+
+    fetch_w.wait()
+    pl.semaphore_wait(barrier, 5 - jnp.where(z == top, 1, 0) - jnp.where(z == 0, 1, 0))
+
+    def rows_of(zo, go, lo, hi):
+        start = ((zo * 2 + k) * 4 + go) * rows + lo
+        return full.at[pl.ds(pl.multiple_of(start, 16), hi - lo), :]
+
+    def copy(kind, zo, go, lo, hi, peer, sent):
+        ref = rows_of(zo, go, lo, hi)
+        return pltpu.make_async_remote_copy(
+            src_ref=ref, dst_ref=ref,
+            send_sem=send_sem.at[sent, zo], recv_sem=recv_sem.at[kind, zo],
+            device_id=peer, device_id_type=MESH)
+
+    me = (g, i)
+    px, py = (gx, i), (gy, i)
+    first_c, first_d = (0, cut_c), (cut_b, rows)
+    spans = {0: (0, rows), 1: first_c, 2: first_d}
+
+    def along(kind, zo, go, up):
+        lo, hi = spans[kind]
+        return copy(kind, zo, go, lo, hi, (g, i + 2 if up else i - 2), kind if up else 7 + kind)
+
+    col = {0: g, 1: gx, 2: gy}
+
+    def spread(kind, do):
+        @pl.when(z < top)
+        def _():
+            do(along(kind, z, col[kind], True))
+
+        @pl.when(z > 0)
+        def _():
+            do(along(kind, z, col[kind], False))
+
+    def forward(kind, zo, do):
+        @pl.when((zo < z) & (z < top))
+        def _():
+            do(along(kind, zo, col[kind], True))
+
+        @pl.when((zo > z) & (z > 0))
+        def _():
+            do(along(kind, zo, col[kind], False))
+
+    start = lambda c: c.start()
+    wait_send = lambda c: c.wait_send()
+
+    def to_x(zo, own):
+        return copy(3, zo, g, 0 if own else cut_c, rows, px, 3)
+
+    def to_y(zo, own):
+        return copy(5, zo, g, 0, rows if own else cut_b, py, 5)
+
+    def diag_x(zo):
+        return copy(4, zo, gy, cut_a, rows, px, 4)
+
+    def diag_y(zo):
+        return copy(6, zo, gx, 0, cut_a, py, 6)
+
+    def got(kind, zo, go, lo, hi):
+        copy(kind, zo, go, lo, hi, px, kind).wait_recv()
+
+    spread(0, start)
+    to_x(z, True).start()
+    to_y(z, True).start()
+
+    fetch_t.wait()
+    steps = features // LANES
+
+    def slabs(c):
+        x = tok[:, pl.ds(pl.multiple_of(c * LANES, LANES), LANES)].astype(jnp.float32)
+        return [x[:, j:j + 128] for j in range(0, LANES, 128)]
+
+    def add_up(c, total):
+        for x in slabs(c):
+            total = total + x
+        return total
+
+    zero = jnp.zeros((count, 128), jnp.float32)
+    mean = jnp.sum(lax.fori_loop(0, steps, add_up, zero), axis=1, keepdims=True) / features
+
+    def squares(c, total):
+        for x in slabs(c):
+            total = total + (x - mean) * (x - mean)
+        return total
+
+    var = jnp.sum(lax.fori_loop(0, steps, squares, zero), axis=1, keepdims=True) / features
+    inv = lax.rsqrt(var + 1e-05)
+
+    def normalize(c, carry):
+        at = pl.ds(pl.multiple_of(c * LANES, LANES), LANES)
+        x = tok[:, at].astype(jnp.float32)
+        norm[0:count, at] = ((x - mean) * inv * gain[:, at] + bias[:, at]).astype(jnp.bfloat16)
+        return carry
+
+    lax.fori_loop(0, steps, normalize, 0)
+
+    other = (g, i + 1 - 2 * k)
+
+    def side(p):
+        at = pl.ds(pl.multiple_of(p * plane + shift * (1 - k), 128), window)
+        return pltpu.make_async_remote_copy(
+            src_ref=norm.at[0:count, at], dst_ref=norm.at[count:2 * count, at],
+            send_sem=side_send.at[p], recv_sem=side_recv.at[p],
+            device_id=other, device_id_type=MESH)
+
+    def side_in(p):
+        at = pl.ds(pl.multiple_of(p * plane + shift * k, 128), window)
+        return pltpu.make_async_remote_copy(
+            src_ref=norm.at[0:count, at], dst_ref=norm.at[count:2 * count, at],
+            send_sem=side_send.at[p], recv_sem=side_recv.at[p],
+            device_id=other, device_id_type=MESH)
+
+    for p in range(planes):
+        side(p).start()
+
+    def product(zo):
+        at = pl.multiple_of(zo * plane + shift * k, 128)
+        return jnp.dot(norm[:, pl.ds(at, window)], full[pl.ds(at, window), :],
+                       preferred_element_type=jnp.float32)
+
+    def whole_in(zo):
+        got(0, zo, g, 0, rows)
+        forward(0, zo, start)
+        to_x(zo, False).start()
+        to_y(zo, False).start()
+
+    def parts_in(zo):
+        got(1, zo, gx, *first_c)
+        forward(1, zo, start)
+        got(2, zo, gy, *first_d)
+        forward(2, zo, start)
+
+    def columns_in(zo):
+        got(3, zo, gx, cut_c, rows)
+        diag_y(zo).start()
+        got(5, zo, gy, 0, cut_b)
+        diag_x(zo).start()
+
+    def diagonal_in(zo):
+        got(4, zo, gxy, cut_a, rows)
+        got(6, zo, gxy, 0, cut_a)
+
+    low = z < (planes // 2)
+
+    def nth(t):
+        mirror = jnp.where(low, z, top - z)
+        pick = jnp.where(t - 1 >= mirror, t, t - 1)
+        return jnp.where(low, pick, top - pick)
+
+    got(3, z, gx, 0, rows)
+    spread(1, start)
+    diag_y(z).start()
+    got(5, z, gy, 0, rows)
+    spread(2, start)
+    diag_x(z).start()
+
+    whole_in(nth(1))
+    for p in range(planes):
+        side_in(p).wait_recv()
+    parts_in(nth(1))
+    columns_in(nth(1))
+    diagonal_in(z)
+    acc[...] = product(z)
+
+    for t in range(2, planes):
+        whole_in(nth(t))
+        parts_in(nth(t))
+        columns_in(nth(t))
+        diagonal_in(nth(t - 1))
+        acc[...] += product(nth(t - 1))
+    diagonal_in(nth(top))
+    acc[...] += product(nth(top))
+
+    last = pltpu.make_async_remote_copy(
+        src_ref=acc.at[count:2 * count, :], dst_ref=part,
+        send_sem=side_send.at[planes], recv_sem=side_recv.at[planes],
+        device_id=other, device_id_type=MESH)
+    last.start()
+
+    for kind in range(3):
+        spread(kind, wait_send)
+    to_x(z, True).wait_send()
+    to_y(z, True).wait_send()
+    diag_x(z).wait_send()
+    diag_y(z).wait_send()
+    for t in range(1, planes):
+        zo = nth(t)
+        for kind in range(3):
+            forward(kind, zo, wait_send)
+        to_x(zo, False).wait_send()
+        to_y(zo, False).wait_send()
+        diag_x(zo).wait_send()
+        diag_y(zo).wait_send()
+    for p in range(planes):
+        side(p).wait_send()
+    last.wait()
+    keys[...] = (acc[0:count, :] + part[...]).astype(keys.dtype)
+
+
+def gathered_keys(weight, tokens, gain, bias, grps, planes):
+    rows, width = weight.shape
+    count, features = tokens.shape
+    unit = 16
+    units = rows // unit
+    cuts = tuple(unit * ((units * n + 3) // 6) for n in (2, 3, 4))
+    anywhere = pl.BlockSpec(memory_space=pl.ANY)
+    vmem = pl.BlockSpec(memory_space=pltpu.VMEM)
+    return pl.pallas_call(
+        functools.partial(gather_kernel, grps, rows, planes, cuts),
+        out_shape=jax.ShapeDtypeStruct((count, width), jnp.bfloat16),
+        in_specs=[anywhere, anywhere, vmem, vmem],
+        out_specs=vmem,
+        scratch_shapes=[
+            pltpu.VMEM((features, width), jnp.bfloat16),
+            pltpu.VMEM((count, features), jnp.bfloat16),
+            pltpu.VMEM((2 * count, features), jnp.bfloat16),
+            pltpu.VMEM((2 * count, width), jnp.float32),
+            pltpu.VMEM((count, width), jnp.float32),
+            pltpu.SemaphoreType.DMA((2,)),
+            pltpu.SemaphoreType.DMA((7, planes)),
+            pltpu.SemaphoreType.DMA((10, planes)),
+            pltpu.SemaphoreType.DMA((planes + 1,)),
+            pltpu.SemaphoreType.DMA((planes + 1,)),
+        ],
+        compiler_params=pltpu.CompilerParams(
+            collective_id=0, has_side_effects=True, vmem_limit_bytes=48 * 2**20),
+        cost_estimate=pl.CostEstimate(
+            flops=2 * count * features * width,
+            bytes_accessed=2 * count * features + 2 * rows * width,
+            transcendentals=0),
+    )(weight, tokens, gain.reshape(1, -1), bias.reshape(1, -1))
+
+
+def kernel_shards(grps, planes, tokens, ln_gain, ln_bias, master, grad, moment1, moment2):
+    new_master, new_moment1, new_moment2, weight = adam(master, grad, moment1, moment2)
+    keys = gathered_keys(weight, tokens, ln_gain, ln_bias, grps, planes)
+    return (new_master, new_moment1, new_moment2, keys)
+
+
 def solution(mesh):
+    grps, members = mesh.shape["grp"], mesh.shape["ing"]
+
+    def body(tokens, ln_gain, ln_bias, master, grad, moment1, moment2):
+        rows, width = master.shape
+        count, features = tokens.shape
+        fits = (
+            grps == 4 and members == 8 and rows % 16 == 0 and rows >= 96
+            and (8 * rows) % 128 == 0 and width % QBLOCK == 0
+            and features % LANES == 0 and count % 16 == 0
+        )
+        plan = functools.partial(kernel_shards, grps, members // 2) if fits else shards
+        return plan(tokens, ln_gain, ln_bias, master, grad, moment1, moment2)
+
     in_specs = (
         P(("grp", "ing"), None),
         P(),
@@ -67,4 +398,4 @@
         P(("ing", "grp"), None),
         P(("grp", "ing"), None),
     )
-    return jax.shard_map(shards, mesh=mesh, in_specs=in_specs, out_specs=out_specs, check_vma=False)
+    return jax.shard_map(body, mesh=mesh, in_specs=in_specs, out_specs=out_specs, check_vma=False)

time: 174 us -> 89.7 us (0.52)
  waiting for transfers between devices: 106 us -> 0 us
  Pallas kernels: 0 us -> 79.6 us
  other arithmetic: 21.3 us -> 0 us
  between operations: 14.1 us -> 0.66 us
  blocking collectives: 8.17 us -> 0 us
  starting transfers between devices: 6.54 us -> 0 us
  matrix products: 5.77 us -> 0 us
  local copies, waits for them, and re-layouts: 11.6 us -> 9.07 us
    pallas_call x0 -> x2, Pallas kernels: none -> 79.6 us  [the longest x1 76.8 us: gathered_keys(): pl.pallas_call(functools.partial(gather_kernel, grps, rows, planes, cuts)...]
    all_to_all x1 -> x0, waiting for transfers between devices: 44.4 us -> none  [shards(): lax.all_to_all(normed, 'ing', split_axis=1, concat_axis=0, tiled=True)]
    reduce_scatter x1 -> x0, waiting for transfers between devices: 34.9 us -> none  [shards(): lax.psum_scatter(jnp.dot(gathered, weight_rows, preferred_element_type=jn...]
    all_gather x1 -> x0, waiting for transfers between devices: 26.7 us -> none  [shards(): lax.all_gather(quant, 'grp', axis=0, tiled=True)]
    convert_element_type x4 -> x0, other arithmetic: 11.6 us -> none  [the longest x1 8.98 us: shards(): (centered * lax.rsqrt(var + 1e-05) * ln_gain + ln_bias).astype(jnp.bfloat16)]
    all_gather x1 -> x0, blocking collectives: 8.17 us -> none  [shards(): lax.all_gather(scale, 'grp', axis=0, tiled=True)]
    all_to_all x1 -> x0, starting transfers between devices: 6.46 us -> none  [shards(): lax.all_to_all(normed, 'ing', split_axis=1, concat_axis=0, tiled=True)]
    dot_general x1 -> x0, matrix products: 5.77 us -> none  [shards(): jnp.dot(gathered, weight_rows, preferred_element_type=jnp.float32)]
  transfers between devices with their start and end apart: 3 -> 0, of which waited for: 3 -> 0; matrix products, arithmetic and copies ran while one was open for 4% -> 0% of each run, Pallas kernels for 0% -> 0%
where the time goes in v1:
time: 89.7 us; the launch traced here: 89.3 us
  Pallas kernels  79.6 us (89%)
  local copies, waits for them, and re-layouts  9.07 us (10%)
    pallas_call x1, Pallas kernels, gathered_keys(): pl.pallas_call(functools.partial(gather_kernel, grps, rows, planes, cuts)...  76.8 us
    unnamed x11, local copies, waits for them, and re-layouts  7.32 us
    pallas_call x1, Pallas kernels, adam(): pl.pallas_call(adam_kernel, grid=(width // QBLOCK,), in_specs=[block] * 4...  2.79 us

profile of v1, /device:TPU:0, one launch (start us, length us, event | category | flops | bytes accessed | tf_op | source)
XLA Modules:
  0.0 89.3 jit_solution(13515204078657731146)
XLA Ops:
  0.6 0.9 reshape.14.gain
  1.5 0.9 reshape.15.bias
  2.4 0.0 copy-start
  2.4 1.2 %copy-done = f32[464,512]{1,0:T(8,128)S(1)} copy-done((f32[464,512]{1,0:T(8,128)S(1)}, f32[464,512]{1,0:T(8,128)}, u32[]{:S(2)}) %copy-start) | copy-done | bytes 950296
  3.6 0.0 copy-start.1
  3.6 1.2 %copy-done.1 = f32[464,512]{1,0:T(8,128)S(1)} copy-done((f32[464,512]{1,0:T(8,128)S(1)}, f32[464,512]{1,0:T(8,128)}, u32[]{:S(2)}) %copy-start.1) | copy-done | bytes 950296
  4.8 0.0 copy-start.2
  4.8 1.2 %copy-done.2 = f32[464,512]{1,0:T(8,128)S(1)} copy-done((f32[464,512]{1,0:T(8,128)S(1)}, f32[464,512]{1,0:T(8,128)}, u32[]{:S(2)}) %copy-start.2) | copy-done | bytes 950296
  6.0 0.0 copy-start.3
  6.0 1.0 %copy-done.3 = bf16[464,512]{1,0:T(8,128)(2,1)S(1)} copy-done((bf16[464,512]{1,0:T(8,128)(2,1)S(1)}, bf16[464,512]{1,0:T(8,128)(2,1)}, u32[]{:S(2)}) %copy-start.3) | copy-done | bytes 475160
  7.0 2.8 %shard_map.102 = (f32[464,512]{1,0:T(8,128)}, f32[464,512]{1,0:T(8,128)}, f32[464,512]{1,0:T(8,128)}, bf16[464,512]{1,0:T(8,128)(2,1)S(1)}) custom-call(f32[464,512]{1,0:T(8,128)S(1)} %copy-done, bf16[464,512]{1,0:T(8,128)(2,1)S(1)} %copy-done.3, f32[464,512]{1,0:T(8,128)S(1)} %copy-done.1, f32[464,512]{1,0:T(8,128)S(1)} %copy-done.2), custom_call_target="tpu_custom_call" | custom-call | tf_op jit(solution)/shard_map/pallas_call | solution.py:80
  9.8 0.0 copy-start.4
  9.8 2.1 %copy-done.4 = bf16[128,14848]{1,0:T(8,128)(2,1)S(1)} copy-done((bf16[128,14848]{1,0:T(8,128)(2,1)S(1)}, bf16[128,14848]{1,0:T(8,128)(2,1)}, u32[]{:S(2)}) %copy-start.4) | copy-done | bytes 3801112
  11.8 76.8 %shard_map.103 = bf16[128,512]{1,0:T(8,128)(2,1)S(1)} custom-call(bf16[464,512]{1,0:T(8,128)(2,1)S(1)} %get-tuple-element.11.weight, bf16[128,14848]{1,0:T(8,128)(2,1)S(1)} %copy-done.4, f32[1,14848]{1,0:T(1,128)S(1)} %reshape.14.gain, f32[1,14848]{1,0:T(1,128)S(1)} %reshape.15.bias), custom_call_target="tpu_custom_call" | custom-call | flops 1946157056 | bytes 4276224 | tf_op jit(solution)/shard_map/pallas_call | solution.py:340
  88.7 0.7 copy.12
Async XLA Ops:
  2.4 1.2 %copy-start = (f32[464,512]{1,0:T(8,128)S(1)}, f32[464,512]{1,0:T(8,128)}, u32[]{:S(2)}) copy-start(f32[464,512]{1,0:T(8,128)} %master.1) | copy-start | bytes 2850820
  3.6 1.2 %copy-start.1 = (f32[464,512]{1,0:T(8,128)S(1)}, f32[464,512]{1,0:T(8,128)}, u32[]{:S(2)}) copy-start(f32[464,512]{1,0:T(8,128)} %moment1.1) | copy-start | bytes 2850820
  4.8 1.2 %copy-start.2 = (f32[464,512]{1,0:T(8,128)S(1)}, f32[464,512]{1,0:T(8,128)}, u32[]{:S(2)}) copy-start(f32[464,512]{1,0:T(8,128)} %moment2.1) | copy-start | bytes 2850820
  6.0 1.0 %copy-start.3 = (bf16[464,512]{1,0:T(8,128)(2,1)S(1)}, bf16[464,512]{1,0:T(8,128)(2,1)}, u32[]{:S(2)}) copy-start(bf16[464,512]{1,0:T(8,128)(2,1)} %grad.1) | copy-start | bytes 1425412
  9.8 2.1 %copy-start.4 = (bf16[128,14848]{1,0:T(8,128)(2,1)S(1)}, bf16[128,14848]{1,0:T(8,128)(2,1)}, u32[]{:S(2)}) copy-start(bf16[128,14848]{1,0:T(8,128)(2,1)} %tokens.1) | copy-start | bytes 11403268

commit v2 on v1

--- a/solution.py
+++ b/solution.py
@@ -83,7 +83,7 @@
         in_specs=[block] * 4,
         out_specs=[block] * 4,
         out_shape=[wide, wide, wide, jax.ShapeDtypeStruct((rows, width), jnp.bfloat16)],
-        compiler_params=pltpu.CompilerParams(vmem_limit_bytes=32 * 2**20),
+        compiler_params=pltpu.CompilerParams(vmem_limit_bytes=60 * 2**20),
     )(master, grad, moment1, moment2)
 
 
@@ -144,56 +144,59 @@
             send_sem=send_sem.at[sent, zo], recv_sem=recv_sem.at[kind, zo],
             device_id=peer, device_id_type=MESH)
 
-    me = (g, i)
     px, py = (gx, i), (gy, i)
-    first_c, first_d = (0, cut_c), (cut_b, rows)
-    spans = {0: (0, rows), 1: first_c, 2: first_d}
-
-    def along(kind, zo, go, up):
-        lo, hi = spans[kind]
-        return copy(kind, zo, go, lo, hi, (g, i + 2 if up else i - 2), kind if up else 7 + kind)
-
-    col = {0: g, 1: gx, 2: gy}
+    spans = {0: (0, cut_a), 1: (0, cut_c), 2: (cut_b, rows), 3: (cut_a, rows)}
+    col = {0: g, 1: gx, 2: gy, 3: g}
+
+    def along(kind, zo, up):
+        peer = (g, i + 2 if up else i - 2)
+        return copy(kind, zo, col[kind], *spans[kind], peer, kind if up else 10 + kind)
 
     def spread(kind, do):
         @pl.when(z < top)
         def _():
-            do(along(kind, z, col[kind], True))
+            do(along(kind, z, True))
 
         @pl.when(z > 0)
         def _():
-            do(along(kind, z, col[kind], False))
+            do(along(kind, z, False))
 
     def forward(kind, zo, do):
         @pl.when((zo < z) & (z < top))
         def _():
-            do(along(kind, zo, col[kind], True))
+            do(along(kind, zo, True))
 
         @pl.when((zo > z) & (z > 0))
         def _():
-            do(along(kind, zo, col[kind], False))
+            do(along(kind, zo, False))
 
     start = lambda c: c.start()
     wait_send = lambda c: c.wait_send()
 
-    def to_x(zo, own):
-        return copy(3, zo, g, 0 if own else cut_c, rows, px, 3)
-
-    def to_y(zo, own):
-        return copy(5, zo, g, 0, rows if own else cut_b, py, 5)
+    own_x = [copy(4, z, g, 0, cut_a, px, 4), copy(5, z, g, cut_a, rows, px, 5)]
+    own_y = [copy(8, z, g, cut_a, rows, py, 8), copy(7, z, g, 0, cut_a, py, 7)]
+
+    def to_x(zo):
+        return copy(4, zo, g, cut_c, rows, px, 4)
+
+    def to_y(zo):
+        return copy(7, zo, g, 0, cut_b, py, 7)
 
     def diag_x(zo):
-        return copy(4, zo, gy, cut_a, rows, px, 4)
+        return copy(6, zo, gy, cut_a, rows, px, 6)
 
     def diag_y(zo):
-        return copy(6, zo, gx, 0, cut_a, py, 6)
+        return copy(9, zo, gx, 0, cut_a, py, 9)
 
     def got(kind, zo, go, lo, hi):
         copy(kind, zo, go, lo, hi, px, kind).wait_recv()
 
     spread(0, start)
-    to_x(z, True).start()
-    to_y(z, True).start()
+    own_x[0].start()
+    own_y[0].start()
+    spread(3, start)
+    own_x[1].start()
+    own_y[1].start()
 
     fetch_t.wait()
     steps = features // LANES
@@ -221,7 +224,7 @@
     def normalize(c, carry):
         at = pl.ds(pl.multiple_of(c * LANES, LANES), LANES)
         x = tok[:, at].astype(jnp.float32)
-        norm[0:count, at] = ((x - mean) * inv * gain[:, at] + bias[:, at]).astype(jnp.bfloat16)
+        norm[0:count, at] = ((x - mean) * inv * gain[at][None, :] + bias[at][None, :]).astype(jnp.bfloat16)
         return carry
 
     lax.fori_loop(0, steps, normalize, 0)
@@ -251,26 +254,28 @@
                        preferred_element_type=jnp.float32)
 
     def whole_in(zo):
-        got(0, zo, g, 0, rows)
+        got(0, zo, g, *spans[0])
         forward(0, zo, start)
-        to_x(zo, False).start()
-        to_y(zo, False).start()
+        got(3, zo, g, *spans[3])
+        forward(3, zo, start)
+        to_x(zo).start()
+        to_y(zo).start()
 
     def parts_in(zo):
-        got(1, zo, gx, *first_c)
+        got(1, zo, gx, *spans[1])
         forward(1, zo, start)
-        got(2, zo, gy, *first_d)
+        got(2, zo, gy, *spans[2])
         forward(2, zo, start)
 
     def columns_in(zo):
-        got(3, zo, gx, cut_c, rows)
+        got(4, zo, gx, cut_c, rows)
         diag_y(zo).start()
-        got(5, zo, gy, 0, cut_b)
+        got(7, zo, gy, 0, cut_b)
         diag_x(zo).start()
 
     def diagonal_in(zo):
-        got(4, zo, gxy, cut_a, rows)
-        got(6, zo, gxy, 0, cut_a)
+        got(6, zo, gxy, cut_a, rows)
+        got(9, zo, gxy, 0, cut_a)
 
     low = z < (planes // 2)
 
@@ -279,27 +284,39 @@
         pick = jnp.where(t - 1 >= mirror, t, t - 1)
         return jnp.where(low, pick, top - pick)
 
-    got(3, z, gx, 0, rows)
-    spread(1, start)
+    end = (z == 0) | (z == top)
+    got(4, z, gx, 0, cut_a)
     diag_y(z).start()
-    got(5, z, gy, 0, rows)
-    spread(2, start)
+    got(8, z, gy, cut_a, rows)
     diag_x(z).start()
-
     whole_in(nth(1))
+
+    @pl.when(end)
+    def _():
+        spread(1, start)
+        spread(2, start)
+
     for p in range(planes):
         side_in(p).wait_recv()
-    parts_in(nth(1))
-    columns_in(nth(1))
+    for t in range(2, top):
+        whole_in(nth(t))
+    got(5, z, gx, cut_a, rows)
+    got(7, z, gy, 0, cut_a)
     diagonal_in(z)
     acc[...] = product(z)
-
-    for t in range(2, planes):
-        whole_in(nth(t))
+    whole_in(nth(top))
+
+    @pl.when(jnp.logical_not(end))
+    def _():
+        spread(1, start)
+        spread(2, start)
+
+    for t in range(1, planes):
         parts_in(nth(t))
         columns_in(nth(t))
-        diagonal_in(nth(t - 1))
-        acc[...] += product(nth(t - 1))
+        if t > 1:
+            diagonal_in(nth(t - 1))
+            acc[...] += product(nth(t - 1))
     diagonal_in(nth(top))
     acc[...] += product(nth(top))
 
@@ -309,20 +326,16 @@
         device_id=other, device_id_type=MESH)
     last.start()
 
-    for kind in range(3):
+    for kind in range(4):
         spread(kind, wait_send)
-    to_x(z, True).wait_send()
-    to_y(z, True).wait_send()
-    diag_x(z).wait_send()
-    diag_y(z).wait_send()
+    for c in own_x + own_y + [diag_x(z), diag_y(z)]:
+        c.wait_send()
     for t in range(1, planes):
         zo = nth(t)
-        for kind in range(3):
+        for kind in range(4):
             forward(kind, zo, wait_send)
-        to_x(zo, False).wait_send()
-        to_y(zo, False).wait_send()
-        diag_x(zo).wait_send()
-        diag_y(zo).wait_send()
+        for c in (to_x(zo), to_y(zo), diag_x(zo), diag_y(zo)):
+            c.wait_send()
     for p in range(planes):
         side(p).wait_send()
     last.wait()
@@ -334,7 +347,8 @@
     count, features = tokens.shape
     unit = 16
     units = rows // unit
-    cuts = tuple(unit * ((units * n + 3) // 6) for n in (2, 3, 4))
+    edge = units // 3
+    cuts = (unit * edge, unit * ((units + 1) // 2), unit * (units - edge))
     anywhere = pl.BlockSpec(memory_space=pl.ANY)
     vmem = pl.BlockSpec(memory_space=pltpu.VMEM)
     return pl.pallas_call(
@@ -349,18 +363,18 @@
             pltpu.VMEM((2 * count, width), jnp.float32),
             pltpu.VMEM((count, width), jnp.float32),
             pltpu.SemaphoreType.DMA((2,)),
-            pltpu.SemaphoreType.DMA((7, planes)),
             pltpu.SemaphoreType.DMA((10, planes)),
+            pltpu.SemaphoreType.DMA((14, planes)),
             pltpu.SemaphoreType.DMA((planes + 1,)),
             pltpu.SemaphoreType.DMA((planes + 1,)),
         ],
         compiler_params=pltpu.CompilerParams(
-            collective_id=0, has_side_effects=True, vmem_limit_bytes=48 * 2**20),
+            collective_id=0, has_side_effects=True, vmem_limit_bytes=60 * 2**20),
         cost_estimate=pl.CostEstimate(
             flops=2 * count * features * width,
             bytes_accessed=2 * count * features + 2 * rows * width,
             transcendentals=0),
-    )(weight, tokens, gain.reshape(1, -1), bias.reshape(1, -1))
+    )(weight, tokens, gain, bias)
 
 
 def kernel_shards(grps, planes, tokens, ln_gain, ln_bias, master, grad, moment1, moment2):

time: 89.7 us -> 72.1 us (0.80)
  Pallas kernels: 79.6 us -> 69.6 us
  local copies, waits for them, and re-layouts: 9.07 us -> 1.57 us
    pallas_call x1, Pallas kernels: 76.8 us -> 64.9 us  [gathered_keys(): pl.pallas_call(functools.partial(gather_kernel, grps, rows, planes, cuts)...]
    unnamed x11 -> x1, local copies, waits for them, and re-layouts: 7.32 us -> 1.57 us
    pallas_call x1, Pallas kernels: 2.79 us -> 4.7 us  [adam(): pl.pallas_call(adam_kernel, grid=(width // QBLOCK,), in_specs=[block] * 4...]
    reshape x2 -> x0, local copies, waits for them, and re-layouts: 1.74 us -> none  [the longest x1 0.87 us: gathered_keys(): bias.reshape(1, -1)]
where the time goes in v2:
time: 72.1 us; the launch traced here: 71.8 us
  Pallas kernels  69.6 us (97%)
  local copies, waits for them, and re-layouts  1.57 us (2%)
    pallas_call x1, Pallas kernels, gathered_keys(): pl.pallas_call(functools.partial(gather_kernel, grps, rows, planes, cuts)...  64.9 us
    pallas_call x1, Pallas kernels, adam(): pl.pallas_call(adam_kernel, grid=(width // QBLOCK,), in_specs=[block] * 4...  4.7 us
    unnamed x1, local copies, waits for them, and re-layouts  1.57 us

profile of v2, /device:TPU:0, one launch (start us, length us, event | category | flops | bytes accessed | tf_op | source)
XLA Modules:
  0.0 71.8 jit_solution(16979212116032757056)
XLA Ops:
  0.6 4.7 %shard_map.102 = (f32[464,512]{1,0:T(8,128)}, f32[464,512]{1,0:T(8,128)}, f32[464,512]{1,0:T(8,128)}, bf16[464,512]{1,0:T(8,128)(2,1)}) custom-call(f32[464,512]{1,0:T(8,128)} %master.1, bf16[464,512]{1,0:T(8,128)(2,1)} %grad.1, f32[464,512]{1,0:T(8,128)} %moment1.1, f32[464,512]{1,0:T(8,128)} %moment2.1), custom_call_target="tpu_custom_call" | custom-call | tf_op jit(solution)/shard_map/pallas_call | solution.py:80
  5.3 64.9 %shard_map.103 = bf16[128,512]{1,0:T(8,128)(2,1)} custom-call(bf16[464,512]{1,0:T(8,128)(2,1)} %get-tuple-element.11.weight, bf16[128,14848]{1,0:T(8,128)(2,1)} %tokens.1, f32[14848]{0:T(1024)} %gain.1, f32[14848]{0:T(1024)} %bias.1), custom_call_target="tpu_custom_call" | custom-call | flops 1946157056 | bytes 4276224 | tf_op jit(solution)/shard_map/pallas_call | solution.py:354
  70.2 1.6 %copy.12 = bf16[128,512]{1,0:T(8,128)(2,1)} copy(bf16[128,512]{1,0:T(8,128)(2,1)} %shard_map.103) | data formatting | bytes 262144

commit v3 on v2

--- a/solution.py
+++ b/solution.py
@@ -62,24 +62,26 @@
     old = master[...]
     first = 0.9 * moment1[...] + 0.1 * gradient
     second = 0.95 * moment2[...] + 0.05 * gradient * gradient
-    step_size = first / 0.19 / (jnp.sqrt(second / 0.0975) + 1e-08)
+    step_size = first * (1 / 0.19) / (jnp.sqrt(second * (1 / 0.0975)) + 1e-08)
     updated = old - 0.008 * (step_size + 0.1 * old)
     out_master[...] = updated
     out_m1[...] = first
     out_m2[...] = second
-    largest = jnp.max(jnp.abs(updated), axis=1, keepdims=True)
-    scale = ((largest + 1e-06) / 127.0).astype(jnp.bfloat16).astype(jnp.float32)
-    quant = (updated / scale).astype(jnp.bfloat16)
-    weight[...] = (quant.astype(jnp.float32) * scale).astype(jnp.bfloat16)
+    for lo in range(0, updated.shape[1], QBLOCK):
+        block = updated[:, lo:lo + QBLOCK]
+        largest = jnp.max(jnp.abs(block), axis=1, keepdims=True)
+        scale = ((largest + 1e-06) / 127.0).astype(jnp.bfloat16).astype(jnp.float32)
+        quant = (block * (1.0 / scale)).astype(jnp.bfloat16)
+        weight[:, lo:lo + QBLOCK] = (quant.astype(jnp.float32) * scale).astype(jnp.bfloat16)
 
 
 def adam(master, grad, moment1, moment2):
     rows, width = master.shape
-    block = pl.BlockSpec((rows, QBLOCK), lambda i: (0, i))
+    block = pl.BlockSpec((rows, 2 * QBLOCK), lambda i: (0, i))
     wide = jax.ShapeDtypeStruct((rows, width), jnp.float32)
     return pl.pallas_call(
         adam_kernel,
-        grid=(width // QBLOCK,),
+        grid=(width // (2 * QBLOCK),),
         in_specs=[block] * 4,
         out_specs=[block] * 4,
         out_shape=[wide, wide, wide, jax.ShapeDtypeStruct((rows, width), jnp.bfloat16)],
@@ -150,7 +152,7 @@
 
     def along(kind, zo, up):
         peer = (g, i + 2 if up else i - 2)
-        return copy(kind, zo, col[kind], *spans[kind], peer, kind if up else 10 + kind)
+        return copy(kind, zo, col[kind], *spans[kind], peer, kind if up else 12 + kind)
 
     def spread(kind, do):
         @pl.when(z < top)
@@ -182,11 +184,19 @@
     def to_y(zo):
         return copy(7, zo, g, 0, cut_b, py, 7)
 
-    def diag_x(zo):
-        return copy(6, zo, gy, cut_a, rows, px, 6)
-
-    def diag_y(zo):
-        return copy(9, zo, gx, 0, cut_a, py, 9)
+    own_diag = [copy(9, z, gx, 0, cut_a, py, 9), copy(6, z, gy, cut_a, rows, px, 6)]
+
+    def part_c(zo):
+        return copy(9, zo, gx, 0, cut_c, py, 9)
+
+    def part_a(zo):
+        return copy(11, zo, gx, cut_c, cut_a, py, 11)
+
+    def part_b(zo):
+        return copy(10, zo, gy, cut_a, cut_b, px, 10)
+
+    def part_d(zo):
+        return copy(6, zo, gy, cut_b, rows, px, 6)
 
     def got(kind, zo, go, lo, hi):
         copy(kind, zo, go, lo, hi, px, kind).wait_recv()
@@ -264,18 +274,22 @@
     def parts_in(zo):
         got(1, zo, gx, *spans[1])
         forward(1, zo, start)
+        part_c(zo).start()
         got(2, zo, gy, *spans[2])
         forward(2, zo, start)
+        part_d(zo).start()
 
     def columns_in(zo):
         got(4, zo, gx, cut_c, rows)
-        diag_y(zo).start()
+        part_a(zo).start()
         got(7, zo, gy, 0, cut_b)
-        diag_x(zo).start()
+        part_b(zo).start()
 
     def diagonal_in(zo):
-        got(6, zo, gxy, cut_a, rows)
-        got(9, zo, gxy, 0, cut_a)
+        got(10, zo, gxy, cut_a, cut_b)
+        got(11, zo, gxy, cut_c, cut_a)
+        got(6, zo, gxy, cut_b, rows)
+        got(9, zo, gxy, 0, cut_c)
 
     low = z < (planes // 2)
 
@@ -286,9 +300,9 @@
 
     end = (z == 0) | (z == top)
     got(4, z, gx, 0, cut_a)
-    diag_y(z).start()
+    own_diag[0].start()
     got(8, z, gy, cut_a, rows)
-    diag_x(z).start()
+    own_diag[1].start()
     whole_in(nth(1))
 
     @pl.when(end)
@@ -302,7 +316,8 @@
         whole_in(nth(t))
     got(5, z, gx, cut_a, rows)
     got(7, z, gy, 0, cut_a)
-    diagonal_in(z)
+    got(6, z, gxy, cut_a, rows)
+    got(9, z, gxy, 0, cut_a)
     acc[...] = product(z)
     whole_in(nth(top))
 
@@ -312,8 +327,8 @@
         spread(2, start)
 
     for t in range(1, planes):
+        columns_in(nth(t))
         parts_in(nth(t))
-        columns_in(nth(t))
         if t > 1:
             diagonal_in(nth(t - 1))
             acc[...] += product(nth(t - 1))
@@ -328,13 +343,13 @@
 
     for kind in range(4):
         spread(kind, wait_send)
-    for c in own_x + own_y + [diag_x(z), diag_y(z)]:
+    for c in own_x + own_y + own_diag:
         c.wait_send()
     for t in range(1, planes):
         zo = nth(t)
         for kind in range(4):
             forward(kind, zo, wait_send)
-        for c in (to_x(zo), to_y(zo), diag_x(zo), diag_y(zo)):
+        for c in (to_x(zo), to_y(zo), part_a(zo), part_b(zo), part_c(zo), part_d(zo)):
             c.wait_send()
     for p in range(planes):
         side(p).wait_send()
@@ -363,8 +378,8 @@
             pltpu.VMEM((2 * count, width), jnp.float32),
             pltpu.VMEM((count, width), jnp.float32),
             pltpu.SemaphoreType.DMA((2,)),
-            pltpu.SemaphoreType.DMA((10, planes)),
-            pltpu.SemaphoreType.DMA((14, planes)),
+            pltpu.SemaphoreType.DMA((12, planes)),
+            pltpu.SemaphoreType.DMA((16, planes)),
             pltpu.SemaphoreType.DMA((planes + 1,)),
             pltpu.SemaphoreType.DMA((planes + 1,)),
         ],

time: 72.1 us -> 70.2 us (0.974)
  Pallas kernels: 69.6 us -> 67.8 us
    pallas_call x1, Pallas kernels: 4.7 us -> 3.69 us  [adam(): pl.pallas_call(adam_kernel, grid=(width // (2 * QBLOCK),), in_specs=[bloc...]
    pallas_call x1, Pallas kernels: 64.9 us -> 64.2 us  [gathered_keys(): pl.pallas_call(functools.partial(gather_kernel, grps, rows, planes, cuts)...]
where the time goes in v3:
time: 70.2 us; the launch traced here: 70 us
  Pallas kernels  67.8 us (97%)
  local copies, waits for them, and re-layouts  1.57 us (2%)
    pallas_call x1, Pallas kernels, gathered_keys(): pl.pallas_call(functools.partial(gather_kernel, grps, rows, planes, cuts)...  64.2 us
    pallas_call x1, Pallas kernels, adam(): pl.pallas_call(adam_kernel, grid=(width // (2 * QBLOCK),), in_specs=[bloc...  3.69 us
    unnamed x1, local copies, waits for them, and re-layouts  1.57 us

profile of v3, /device:TPU:0, one launch (start us, length us, event | category | flops | bytes accessed | tf_op | source)
XLA Modules:
  0.0 70.0 jit_solution(6396694836632934844)
XLA Ops:
  0.6 3.7 %shard_map.102 = (f32[464,512]{1,0:T(8,128)}, f32[464,512]{1,0:T(8,128)}, f32[464,512]{1,0:T(8,128)}, bf16[464,512]{1,0:T(8,128)(2,1)}) custom-call(f32[464,512]{1,0:T(8,128)} %master.1, bf16[464,512]{1,0:T(8,128)(2,1)} %grad.1, f32[464,512]{1,0:T(8,128)} %moment1.1, f32[464,512]{1,0:T(8,128)} %moment2.1), custom_call_target="tpu_custom_call" | custom-call | tf_op jit(solution)/shard_map/pallas_call | solution.py:82
  4.3 64.2 %shard_map.103 = bf16[128,512]{1,0:T(8,128)(2,1)} custom-call(bf16[464,512]{1,0:T(8,128)(2,1)} %get-tuple-element.11.weight, bf16[128,14848]{1,0:T(8,128)(2,1)} %tokens.1, f32[14848]{0:T(1024)} %gain.1, f32[14848]{0:T(1024)} %bias.1), custom_call_target="tpu_custom_call" | custom-call | flops 1946157056 | bytes 4276224 | tf_op jit(solution)/shard_map/pallas_call | solution.py:369
  68.5 1.6 %copy.12 = bf16[128,512]{1,0:T(8,128)(2,1)} copy(bf16[128,512]{1,0:T(8,128)(2,1)} %shard_map.103) | data formatting | bytes 262144

commit v4 on v3

--- a/solution.py
+++ b/solution.py
@@ -363,7 +363,7 @@
     unit = 16
     units = rows // unit
     edge = units // 3
-    cuts = (unit * edge, unit * ((units + 1) // 2), unit * (units - edge))
+    cuts = (unit * (edge - 1), unit * ((units + 1) // 2), unit * (units - edge))
     anywhere = pl.BlockSpec(memory_space=pl.ANY)
     vmem = pl.BlockSpec(memory_space=pltpu.VMEM)
     return pl.pallas_call(

time: 70.2 us -> 69.9 us (level)
  no operation moved by 1% of the time
where the time goes in v4:
time: 69.9 us; the launch traced here: 69.7 us
  Pallas kernels  67.5 us (97%)
  local copies, waits for them, and re-layouts  1.57 us (2%)
    pallas_call x1, Pallas kernels, gathered_keys(): pl.pallas_call(functools.partial(gather_kernel, grps, rows, planes, cuts)...  63.8 us
    pallas_call x1, Pallas kernels, adam(): pl.pallas_call(adam_kernel, grid=(width // (2 * QBLOCK),), in_specs=[bloc...  3.69 us
    unnamed x1, local copies, waits for them, and re-layouts  1.57 us

profile of v4, /device:TPU:0, one launch (start us, length us, event | category | flops | bytes accessed | tf_op | source)
XLA Modules:
  0.0 69.7 jit_solution(7129856559712738585)
XLA Ops:
  0.6 3.7 %shard_map.102 = (f32[464,512]{1,0:T(8,128)}, f32[464,512]{1,0:T(8,128)}, f32[464,512]{1,0:T(8,128)}, bf16[464,512]{1,0:T(8,128)(2,1)}) custom-call(f32[464,512]{1,0:T(8,128)} %master.1, bf16[464,512]{1,0:T(8,128)(2,1)} %grad.1, f32[464,512]{1,0:T(8,128)} %moment1.1, f32[464,512]{1,0:T(8,128)} %moment2.1), custom_call_target="tpu_custom_call" | custom-call | tf_op jit(solution)/shard_map/pallas_call | solution.py:82
  4.3 63.8 %shard_map.103 = bf16[128,512]{1,0:T(8,128)(2,1)} custom-call(bf16[464,512]{1,0:T(8,128)(2,1)} %get-tuple-element.11.weight, bf16[128,14848]{1,0:T(8,128)(2,1)} %tokens.1, f32[14848]{0:T(1024)} %gain.1, f32[14848]{0:T(1024)} %bias.1), custom_call_target="tpu_custom_call" | custom-call | flops 1946157056 | bytes 4276224 | tf_op jit(solution)/shard_map/pallas_call | solution.py:369
  68.2 1.6 %copy.12 = bf16[128,512]{1,0:T(8,128)(2,1)} copy(bf16[128,512]{1,0:T(8,128)(2,1)} %shard_map.103) | data formatting | bytes 262144
